TPU v7x, 32 devices: a whole 2x2x4 slice. The times are simulated.
32 devices in a mesh: dp: 8 (over z, y), seq: 4 (over x, core).
Axes of the slice: x: 2, y: 2, z: 4, core: 2. Of those that a mesh axis runs over, the one named last changes fastest.
Arguments:
- latents: bfloat16 [16384, 3072], P(('dp', 'seq')), may hold values from -6 to 6
- target: int32 [16384], P(('dp', 'seq')), may hold values from 0 to 16383, as said below
- segment_ids: int32 [8, 2048], P('dp', 'seq'), may hold values from 0 to 7, never falling along the last dimension, each value on 1 to 512 neighbouring positions
- clip_bucket: int32 [8, 8], P('dp'), may hold values from 0 to 15
- mod_table: bfloat16 [16, 6144], replicated, may hold values from -3 to 3
- w_query: bfloat16 [3072, 1536], P('dp', 'seq')
- w_key: bfloat16 [3072, 1536], P('dp', 'seq')
- w_value: bfloat16 [3072, 1536], P('dp', 'seq'), may hold values from -0.109375 to 0.109375
Outputs:
- attended: bfloat16 [16384, 1536], P(('dp', 'seq'))
Inputs may be any that keep to these rules, and one draw needn't show every extreme that they name: `target`: a permutation of 0 to 16383; a token stays at the same index of seq; a device sends at most 96 tokens to one index of dp, exactly 96 to some index in every draw, and sends to at most (607) // 96 + 1 indices.
All inputs are finite; a program needn't handle non-finite values.
Results may differ from a plain program's by a relative error of at most 0.0051.
Values may be sent and summed in bfloat16 or wider, within the bound.
No kernel may reach another device: no remote copies, remote signals or barrier semaphores. Data moves between devices by JAX's collectives and lax.ppermute only.
A program may use at most 128 MiB of HBM per device.

v0:
```python
import jax
import jax.numpy as jnp
from jax import lax
from jax.sharding import PartitionSpec as P

HEAD_DIM = 128


def modulated_norm(latent_rows, segment_row, bucket_row, mod_table):
    clip_count = bucket_row.shape[0]
    bucket_count = mod_table.shape[0]
    width = latent_rows.shape[1]
    clip_hit = segment_row[:, None] == jnp.arange(clip_count, dtype=jnp.int32)[None, :]
    token_bucket = jnp.sum(jnp.where(clip_hit, bucket_row[None, :], 0), axis=1)
    bucket_hit = (
        token_bucket[:, None] == jnp.arange(bucket_count, dtype=jnp.int32)[None, :]
    ).astype(jnp.bfloat16)
    modulation = jnp.dot(bucket_hit, mod_table, preferred_element_type=jnp.float32)
    shift_part = modulation[:, :width]
    scale_part = modulation[:, width:]
    widened = latent_rows.astype(jnp.float32)
    row_mean = jnp.mean(widened, axis=1, keepdims=True)
    centered = widened - row_mean
    row_var = jnp.mean(centered * centered, axis=1, keepdims=True)
    normalized = centered * lax.rsqrt(row_var + 1e-06)
    return (normalized * (1.0 + scale_part) + shift_part).astype(jnp.bfloat16)


def project_three(hidden_rows, pieces):
    return (
        jnp.dot(hidden_rows, pieces[0], preferred_element_type=jnp.float32),
        jnp.dot(hidden_rows, pieces[1], preferred_element_type=jnp.float32),
        jnp.dot(hidden_rows, pieces[2], preferred_element_type=jnp.float32),
    )


def attend(query_rows, key_rows, value_rows, sequence_clips):
    length = query_rows.shape[0]
    heads_here = query_rows.shape[1] // HEAD_DIM
    block_rows = min(512, length)
    block_count = length // block_rows
    factor = HEAD_DIM ** (-0.5)
    query_blocks = query_rows.reshape(block_count, block_rows, heads_here, HEAD_DIM)
    clip_blocks = sequence_clips.reshape(block_count, block_rows)
    key_heads = key_rows.reshape(length, heads_here, HEAD_DIM)
    value_heads = value_rows.reshape(length, heads_here, HEAD_DIM)

    def attend_block(blocks):
        query_block, clip_block = blocks
        scores = (
            jnp.einsum("qhd,khd->hqk", query_block, key_heads, preferred_element_type=jnp.float32)
            * factor
        )
        same_clip = clip_block[:, None] == sequence_clips[None, :]
        scores = jnp.where(same_clip[None, :, :], scores, -1e30)
        row_max = jnp.max(scores, axis=2, keepdims=True)
        exponent = jnp.exp(scores - row_max)
        row_total = jnp.sum(exponent, axis=2, keepdims=True)
        weights_bf = (exponent / row_total).astype(jnp.bfloat16)
        result = jnp.einsum(
            "hqk,khd->qhd", weights_bf, value_heads, preferred_element_type=jnp.float32
        )
        return result.reshape(block_rows, heads_here * HEAD_DIM).astype(jnp.bfloat16)

    outcome = lax.map(attend_block, (query_blocks, clip_blocks))
    return outcome.reshape(length, heads_here * HEAD_DIM)


def on_device(latents, target, segment_ids, clip_bucket, mod_table, w_query, w_key, w_value):
    local_rows = latents.shape[0]
    width = latents.shape[1]
    group_count = lax.axis_size("dp")
    seq_count = lax.axis_size("seq")
    capacity = max(2, 3 * local_rows // (2 * group_count))
    dest_device = target // (seq_count * local_rows)
    dest_row = target % local_rows
    device_hit = (dest_device[:, None] == jnp.arange(group_count, dtype=jnp.int32)[None, :]).astype(
        jnp.int32
    )
    earlier = jnp.cumsum(device_hit, axis=0) - device_hit
    rank_row = jnp.sum(earlier * device_hit, axis=1)
    send_slot = dest_device * capacity + rank_row
    outgoing = jnp.zeros((group_count * capacity, width), jnp.bfloat16).at[send_slot].set(latents)
    outgoing_rows = (
        jnp.full((group_count * capacity,), local_rows, jnp.int32).at[send_slot].set(dest_row)
    )
    incoming, incoming_rows = (
        lax.all_to_all(outgoing, "dp", split_axis=0, concat_axis=0, tiled=True),
        lax.all_to_all(outgoing_rows, "dp", split_axis=0, concat_axis=0, tiled=True),
    )
    placed = (
        jnp.zeros((local_rows, width), jnp.bfloat16).at[incoming_rows].set(incoming, mode="drop")
    )
    hidden = modulated_norm(placed, segment_ids[0], clip_bucket[0], mod_table)
    columns_full = (
        lax.all_gather(w_query, "seq", axis=1, tiled=True),
        lax.all_gather(w_key, "seq", axis=1, tiled=True),
        lax.all_gather(w_value, "seq", axis=1, tiled=True),
    )
    query_f, key_f, value_f = project_three(
        hidden,
        (
            lax.all_gather(columns_full[0], "dp", axis=0, tiled=True),
            lax.all_gather(columns_full[1], "dp", axis=0, tiled=True),
            lax.all_gather(columns_full[2], "dp", axis=0, tiled=True),
        ),
    )
    query_rows, key_rows, value_rows = (
        lax.all_to_all(
            query_f.astype(jnp.bfloat16), "seq", split_axis=1, concat_axis=0, tiled=True
        ),
        lax.all_to_all(key_f.astype(jnp.bfloat16), "seq", split_axis=1, concat_axis=0, tiled=True),
        lax.all_to_all(
            value_f.astype(jnp.bfloat16), "seq", split_axis=1, concat_axis=0, tiled=True
        ),
    )
    sequence_clips = lax.all_gather(segment_ids, "seq", axis=1, tiled=True)[0]
    head_output = attend(query_rows, key_rows, value_rows, sequence_clips)
    return lax.all_to_all(head_output, "seq", split_axis=0, concat_axis=1, tiled=True)


def solution(mesh):
    in_specs = (
        P(("dp", "seq"), None),
        P(("dp", "seq")),
        P("dp", "seq"),
        P("dp", None),
        P(),
        P("dp", "seq"),
        P("dp", "seq"),
        P("dp", "seq"),
    )
    out_specs = P(("dp", "seq"), None)
    return jax.shard_map(
        on_device, mesh=mesh, in_specs=in_specs, out_specs=out_specs, check_vma=False
    )
```

profile of v0, /device:TPU:0, one launch (start us, length us, event | category | flops | bytes accessed | tf_op | source)
XLA Modules:
  0.0 733.8 jit_solution(1478769290769905878)
XLA Ops:
  6.5 0.7 all-gather.11.cloned.1.call-update
  7.3 0.7 all-gather.15.cloned.1.call-update
  8.1 0.7 all-gather.7.cloned.1.call-update
  8.8 20.3 %all-gather.11.cloned.1.call-done = bf16[384,1536]{1,0:T(8,128)(2,1)} async-done(((bf16[384,384]{1,0:T(8,128)(2,1)}), bf16[384,1536]{1,0:T(8,128)(2,1)}) %all-gather.11.cloned.1.call-update) | async-done | bytes 1179664 | tf_op jit(solution)/shard_map/all_gather | solution.py:97
  29.2 19.0 %all-gather.15.cloned.1.call-done = bf16[384,1536]{1,0:T(8,128)(2,1)} async-done(((bf16[384,384]{1,0:T(8,128)(2,1)}), bf16[384,1536]{1,0:T(8,128)(2,1)}) %all-gather.15.cloned.1.call-update) | async-done | bytes 1179664 | tf_op jit(solution)/shard_map/all_gather | solution.py:98
  48.2 19.0 %all-gather.7.cloned.1.call-done = bf16[384,1536]{1,0:T(8,128)(2,1)} async-done(((bf16[384,384]{1,0:T(8,128)(2,1)}), bf16[384,1536]{1,0:T(8,128)(2,1)}) %all-gather.7.cloned.1.call-update) | async-done | bytes 1179664 | tf_op jit(solution)/shard_map/all_gather | solution.py:96
  67.3 1.1 reduce-window.6
  68.8 2.4 scatter_custom_fusion
  71.9 5.5 all-to-all-start
  77.4 9.3 %scatter_custom_fusion.1 = bf16[768,3072]{1,0:T(8,128)(2,1)} fusion(s32[512]{0:T(512)S(1)} %compare_select_fusion.1, bf16[512,3072]{1,0:T(8,128)(2,1)} %param.10, bf16[]{:T(256)} %constant.62.clone.1), kind=kCustom, calls=%fused_computation.38 | custom fusion | bytes 4719104 | tf_op jit(solution)/shard_map/scatter | solution.py:83
  86.7 6.4 all-to-all-start.1
  93.2 6.4 fusion.36
  100.9 183.5 %all-to-all-done.1 = bf16[8,96,3072]{2,1,0:T(8,128)(2,1)} async-done(((bf16[8,96,3072]{2,1,0:T(8,128)(2,1)}), bf16[8,96,3072]{2,1,0:T(8,128)(2,1)}, u32[]{:S(2)}, u32[]{:S(2)}) %all-to-all-start.1) | async-done | bytes 4718624 | tf_op jit(solution)/shard_map/all_to_all | solution.py:88
  284.4 11.7 %scatter_custom_fusion.2 = bf16[512,3072]{1,0:T(8,128)(2,1)S(1)} fusion(s32[768]{0:T(1024)S(1)} %fusion.41, bf16[768,3072]{1,0:T(8,128)(2,1)} %bitcast.10, bf16[]{:T(256)} %constant.62.clone.1), kind=kCustom, calls=%fused_computation.41 | custom fusion | bytes 3146240 | tf_op jit(solution)/shard_map/scatter | solution.py:92
  296.5 1.0 fusion.28
  297.5 7.0 fusion.31
  304.5 10.6 %convolution_convert_fusion.1 = bf16[512,1536]{1,0:T(8,128)(2,1)S(1)} fusion(bf16[512,3072]{1,0:T(8,128)(2,1)} %fusion.31, bf16[3072,1536]{1,0:T(8,128)(2,1)} %all-gather.13.cloned.1.call-done), kind=kOutput, calls=%fused_computation.36 | convolution fusion | flops 4832624640 | bytes 14155776 | tf_op jit(solution)/shard_map/dot_general | solution.py:32
  315.1 1.6 copy.36
  316.7 3.6 all-to-all-start.3
  320.2 116.4 %all-gather.17.cloned.1.call-done = bf16[3072,1536]{1,0:T(8,128)(2,1)} async-done(((bf16[384,1536]{1,0:T(8,128)(2,1)}), bf16[3072,1536]{1,0:T(8,128)(2,1)}) %all-gather.17.cloned.1.call-update) | async-done | bytes 9437200 | tf_op jit(solution)/shard_map/all_gather | solution.py:105
  436.7 9.4 %convolution_convert_fusion = bf16[512,1536]{1,0:T(8,128)(2,1)S(1)} fusion(bf16[512,3072]{1,0:T(8,128)(2,1)} %fusion.31, bf16[3072,1536]{1,0:T(8,128)(2,1)} %all-gather.17.cloned.1.call-done), kind=kOutput, calls=%fused_computation.35 | convolution fusion | flops 4832624640 | bytes 14155776 | tf_op jit(solution)/shard_map/dot_general | solution.py:33
  446.0 1.3 copy.41
  447.4 3.6 all-to-all-start.4
  450.9 124.0 %all-gather.9.cloned.1.call-done = bf16[3072,1536]{1,0:T(8,128)(2,1)} async-done(((bf16[384,1536]{1,0:T(8,128)(2,1)}), bf16[3072,1536]{1,0:T(8,128)(2,1)}) %all-gather.9.cloned.1.call-update) | async-done | bytes 9437200 | tf_op jit(solution)/shard_map/all_gather | solution.py:103
  575.0 10.3 %convolution_convert_fusion.2 = bf16[512,1536]{1,0:T(8,128)(2,1)} fusion(bf16[512,3072]{1,0:T(8,128)(2,1)} %fusion.31, bf16[3072,1536]{1,0:T(8,128)(2,1)} %all-gather.9.cloned.1.call-done), kind=kOutput, calls=%fused_computation.37 | convolution fusion | flops 4832624640 | bytes 14155776 | tf_op jit(solution)/shard_map/dot_general | solution.py:31
  585.2 2.6 copy.35
  587.8 4.4 all-to-all-start.2
  592.2 21.0 %all_gather.21 = s32[1,2048]{1,0:T(1,128)S(1)} all-gather(s32[1,512]{1,0:T(1,128)S(1)} %copy-done.3), channel_id=1, replica_groups=mesh['dp'=8,'seq'=4] {'seq'}, dimensions={1}, use_global_device_ids=true | all-gather | bytes 10240 | tf_op jit(solution)/shard_map/all_gather | solution.py:117
  613.9 2.4 copy.29
  616.3 2.8 reshape.135
  619.1 1.6 copy.33
  620.7 1.5 copy.31
  622.2 2.4 reshape.136
  624.6 76.6 %while.10 = (s32[]{:T(128)}, bf16[4,512,384]{1,2,0:T(8,128)(2,1)}, s32[4,512]{1,0:T(4,128)S(1)}, s32[1,2048]{1,0:T(1,128)S(1)}, bf16[4,512,3,128]{1,3,2,0:T(8,12...) while((s32[]{:T(128)}, bf16[4,512,384]{1,2,0:T(8,128)(2,1)}, ...), condition=%wide.region_12.13_spmd, body=%wide.region_9.12_spmd.sunk | while | flops 1630734336 | bytes 32009304 | solution.py:65
  625.3 10.4 %fusion.69 = (f32[3,512]{1,0:T(4,128)S(1)}, f32[3,512,2048]{2,1,0:T(8,128)}) fusion(pred[512,2048]{1,0:T(8,128)(4,1)S(1)} %broadcast_compare_fusion.2, bf16[2048,3,128]{2,0,1:T(8,128)(2,1)S(1)} %get-tuple-element.150, bf16[4,512,3,128]{1,3,2,0:T(8,128)(2,1)} %get-tuple-element.149, s32[]{:T(128)} %get-tuple-element.137), kind=kOutput, calls=%fused_computation.71.clone.1 | convolution fusion | flops 817891328 | bytes 15604224 | tf_op jit(solution)/shard_map/while/body/eval_jaxpr/sub | solution.py:57
  635.7 7.3 fusion.70
  643.0 0.8 bitcast_dynamic-update-slice_fusion.2
  644.4 10.4 %fusion.69 = (f32[3,512]{1,0:T(4,128)S(1)}, f32[3,512,2048]{2,1,0:T(8,128)}) fusion(pred[512,2048]{1,0:T(8,128)(4,1)S(1)} %broadcast_compare_fusion.2, bf16[2048,3,128]{2,0,1:T(8,128)(2,1)S(1)} %get-tuple-element.150, bf16[4,512,3,128]{1,3,2,0:T(8,128)(2,1)} %get-tuple-element.149, s32[]{:T(128)} %get-tuple-element.137), kind=kOutput, calls=%fused_computation.71.clone.1 | convolution fusion | flops 817891328 | bytes 15604224 | tf_op jit(solution)/shard_map/while/body/eval_jaxpr/sub | solution.py:57
  654.8 7.3 fusion.70
  662.1 0.8 bitcast_dynamic-update-slice_fusion.2
  663.6 10.4 %fusion.69 = (f32[3,512]{1,0:T(4,128)S(1)}, f32[3,512,2048]{2,1,0:T(8,128)}) fusion(pred[512,2048]{1,0:T(8,128)(4,1)S(1)} %broadcast_compare_fusion.2, bf16[2048,3,128]{2,0,1:T(8,128)(2,1)S(1)} %get-tuple-element.150, bf16[4,512,3,128]{1,3,2,0:T(8,128)(2,1)} %get-tuple-element.149, s32[]{:T(128)} %get-tuple-element.137), kind=kOutput, calls=%fused_computation.71.clone.1 | convolution fusion | flops 817891328 | bytes 15604224 | tf_op jit(solution)/shard_map/while/body/eval_jaxpr/sub | solution.py:57
  674.0 7.3 fusion.70
  681.3 0.8 bitcast_dynamic-update-slice_fusion.2
  682.7 10.4 %fusion.69 = (f32[3,512]{1,0:T(4,128)S(1)}, f32[3,512,2048]{2,1,0:T(8,128)}) fusion(pred[512,2048]{1,0:T(8,128)(4,1)S(1)} %broadcast_compare_fusion.2, bf16[2048,3,128]{2,0,1:T(8,128)(2,1)S(1)} %get-tuple-element.150, bf16[4,512,3,128]{1,3,2,0:T(8,128)(2,1)} %get-tuple-element.149, s32[]{:T(128)} %get-tuple-element.137), kind=kOutput, calls=%fused_computation.71.clone.1 | convolution fusion | flops 817891328 | bytes 15604224 | tf_op jit(solution)/shard_map/while/body/eval_jaxpr/sub | solution.py:57
  693.1 7.3 fusion.70
  700.4 0.8 bitcast_dynamic-update-slice_fusion.2
  701.2 23.7 %all_to_all.88 = bf16[4,512,384]{1,2,0:T(8,128)(2,1)S(1)} all-to-all(bf16[4,512,384]{1,2,0:T(8,128)(2,1)} %get-tuple-element.42), channel_id=1, replica_groups=mesh['dp'=8,'seq'=4] {'seq'}, dimensions={0} | all-to-all | bytes 3145728 | tf_op jit(solution)/shard_map/all_to_all | solution.py:119
  725.0 1.6 copy.37
  (53 shorter events, 6.5 us)
Async XLA Ops:
  6.5 86.7 %copy-start = (bf16[16,6144]{1,0:T(8,128)(2,1)S(1)}, bf16[16,6144]{1,0:T(8,128)(2,1)}, u32[]{:S(2)}) copy-start(bf16[16,6144]{1,0:T(8,128)(2,1)} %param.14) | copy-start | bytes 589828
  6.5 60.7 %copy-start.4 = (s32[512]{0:T(512)S(1)}, s32[512]{0:T(512)}, u32[]{:S(2)}) copy-start(s32[512]{0:T(512)} %param.11) | copy-start | bytes 6148
  6.5 22.6 %all-gather.11.cloned.1.call-start = ((), (), s32[]{:S(2)}) async-start(), calls=%async_computation.8 | async-start | bytes 1474560 | tf_op jit(solution)/shard_map/all_gather | solution.py:97
  7.3 40.9 %all-gather.15.cloned.1.call-start = ((), (), s32[]{:S(2)}) async-start(), calls=%async_computation.10 | async-start | bytes 1474560 | tf_op jit(solution)/shard_map/all_gather | solution.py:98
  8.0 59.2 %all-gather.7.cloned.1.call-start = ((), (), s32[]{:S(2)}) async-start(), calls=%async_computation.6 | async-start | bytes 1474560 | tf_op jit(solution)/shard_map/all_gather | solution.py:96
  8.7 295.8 %all-gather.13.cloned.1.call-start = ((), (), s32[]{:S(2)}) async-start(), calls=%async_computation.9 | async-start | bytes 10616832 | tf_op jit(solution)/shard_map/all_gather | solution.py:104
  29.1 407.5 %all-gather.17.cloned.1.call-start = ((), (), s32[]{:S(2)}) async-start(), calls=%async_computation.11 | async-start | bytes 10616832 | tf_op jit(solution)/shard_map/all_gather | solution.py:105
  48.2 526.8 %all-gather.9.cloned.1.call-start = ((), (), s32[]{:S(2)}) async-start(), calls=%async_computation.7 | async-start | bytes 10616832 | tf_op jit(solution)/shard_map/all_gather | solution.py:103
  71.9 14.8 %all-to-all-start = ((s32[8,96,1]{1,2,0:T(1,128)}), s32[8,96,1]{1,2,0:T(1,128)S(1)}, u32[]{:S(2)}, u32[]{:S(2)}) async-start(s32[8,96,1]{1,2,0:T(1,128)} %bitcast.8), calls=%async_computation | async-start | bytes 8192 | tf_op jit(solution)/shard_map/all_to_all | solution.py:89
  86.7 6.4 copy-start.3
  86.7 6.4 copy-start.5
  86.7 197.7 %all-to-all-start.1 = ((bf16[8,96,3072]{2,1,0:T(8,128)(2,1)}), bf16[8,96,3072]{2,1,0:T(8,128)(2,1)}, u32[]{:S(2)}, u32[]{:S(2)}) async-start(bf16[8,96,3072]{2,1,0:T(8,128)(2,1)} %bitcast.76), calls=%async_computation.1 | async-start | bytes 9437184 | tf_op jit(solution)/shard_map/all_to_all | solution.py:88
  316.7 130.7 %all-to-all-start.3 = ((bf16[512,4,384]{0,2,1:T(8,128)(2,1)}), bf16[512,4,384]{0,2,1:T(8,128)(2,1)S(1)}, u32[]{:S(2)}, u32[]{:S(2)}) async-start(bf16[512,4,384]{0,2,1:T(8,128)(2,1)} %bitcast.16), calls=%async_computation.3 | async-start | bytes 3145728 | tf_op jit(solution)/shard_map/all_to_all | solution.py:112
  447.4 140.5 %all-to-all-start.4 = ((bf16[512,4,384]{2,0,1:T(8,128)(2,1)}), bf16[512,4,384]{2,0,1:T(8,128)(2,1)S(1)}, u32[]{:S(2)}, u32[]{:S(2)}) async-start(bf16[512,4,384]{2,0,1:T(8,128)(2,1)} %bitcast.81), calls=%async_computation.4 | async-start | bytes 3145728 | tf_op jit(solution)/shard_map/all_to_all | solution.py:113
  587.8 36.8 %all-to-all-start.2 = ((bf16[512,4,384]{0,2,1:T(8,128)(2,1)}), bf16[512,4,384]{0,2,1:T(8,128)(2,1)}, u32[]{:S(2)}, u32[]{:S(2)}) async-start(bf16[512,4,384]{0,2,1:T(8,128)(2,1)} %bitcast.80), calls=%async_computation.2 | async-start | bytes 3145728 | tf_op jit(solution)/shard_map/all_to_all | solution.py:109
  622.2 2.4 copy-start.2
  701.2 25.3 %copy-start.1 = (bf16[16,6144]{1,0:T(8,128)(2,1)S(1)}, bf16[16,6144]{1,0:T(8,128)(2,1)}, u32[]{:S(2)}) copy-start(bf16[16,6144]{1,0:T(8,128)(2,1)} %param.14) | copy-start | bytes 589828
Sparse Core Ops, SparseCore 0:
  8.9 20.1 all-gather.10
  30.7 17.4 all-gather.14
  49.7 17.4 all-gather.6
  69.2 228.8 all-gather.12
  300.1 136.4 all-gather.16
  438.7 136.2 all-gather.8
where the time goes:
time: 741 us; the launch traced here: 734 us
  waiting for transfers between devices  484 us (65%)
  matrix products  107 us (14%)
  local copies, waits for them, and re-layouts  45.8 us (6%)
  blocking collectives  44.8 us (6%)
  starting transfers between devices  23.6 us (3%)
  between operations  14.1 us (2%)
  other arithmetic  13.7 us (2%)
    all_to_all x1, waiting for transfers between devices, on_device(): lax.all_to_all(outgoing, 'dp', split_axis=0, concat_axis=0, tiled=True)  183 us
    all_gather x1, waiting for transfers between devices, on_device(): lax.all_gather(columns_full[0], 'dp', axis=0, tiled=True)  124 us
    all_gather x1, waiting for transfers between devices, on_device(): lax.all_gather(columns_full[2], 'dp', axis=0, tiled=True)  116 us
    sub x4, matrix products, attend_block(): exponent = jnp.exp(scores - row_max)  41.7 us
    dot_general x4, matrix products, attend_block(): jnp.einsum('hqk,khd->qhd', weights_bf, value_heads, preferred_element_typ...  29.1 us
    all_to_all x1, blocking collectives, on_device(): lax.all_to_all(head_output, 'seq', split_axis=0, concat_axis=1, tiled=True)  23.7 us
    all_gather x1, blocking collectives, on_device(): sequence_clips = lax.all_gather(segment_ids, 'seq', axis=1, tiled=True)[0]  21 us
    all_gather x1, waiting for transfers between devices, on_device(): lax.all_gather(w_key, 'seq', axis=1, tiled=True)  20.3 us
  transfers between devices with their start and end apart: 11, of which 6 were waited for; matrix products, arithmetic and copies ran while one was open for 12% of the time, Pallas kernels for 0%

commit v1 on v0

v1 whole, which is shorter than its diff:
```python
import functools

import jax
import jax.numpy as jnp
from jax import lax
from jax.experimental import pallas as pl
from jax.experimental.pallas import tpu as pltpu
from jax.sharding import PartitionSpec as P

HEAD_DIM = 128
TILE = 256
LANES = 128
MOST = 512
BLOCKED = -(2.0**100)


def params(mebibytes):
    return pltpu.CompilerParams(vmem_limit_bytes=mebibytes * 1024 * 1024)


def cost(flops, moved):
    return pl.CostEstimate(flops=int(flops), bytes_accessed=int(moved), transcendentals=0)


def one_hot(found):
    return found.astype(jnp.float32).astype(jnp.bfloat16)


def pack_kernel(me_ref, target_ref, latents_ref, *out_refs, seq_count):
    group_count = len(out_refs)
    capacity = out_refs[0].shape[0]
    local_rows, width = latents_ref.shape
    target = target_ref[...]
    dest = target // (seq_count * local_rows)
    row = target % local_rows
    groups = lax.broadcasted_iota(jnp.int32, (max(16, group_count), local_rows), 0)
    hit = (groups == dest).astype(jnp.float32)
    before = lax.broadcasted_iota(jnp.int32, (local_rows, local_rows), 0)
    after = lax.broadcasted_iota(jnp.int32, (local_rows, local_rows), 1)
    ranks = jnp.dot(
        hit.astype(jnp.bfloat16), one_hot(before < after), preferred_element_type=jnp.float32
    )
    rank = jnp.sum(hit * ranks, axis=0, keepdims=True).astype(jnp.int32)
    slots = lax.bitwise_xor(dest, me_ref[0]) * capacity + rank
    wanted = lax.broadcasted_iota(jnp.int32, (group_count * capacity, local_rows), 0)
    pick = one_hot(wanted == slots)
    lines = lax.broadcasted_iota(jnp.int32, (LANES, local_rows), 0)
    places = jnp.where(lines == 0, row // 16, jnp.where(lines == 1, row % 16, 1))
    places = places.astype(jnp.float32).astype(jnp.bfloat16)

    def store(columns, result):
        result = result.astype(jnp.bfloat16)
        for relative, out_ref in enumerate(out_refs):
            out_ref[:, columns] = result[relative * capacity : (relative + 1) * capacity]

    store(
        slice(width, width + LANES),
        lax.dot_general(pick, places, (((1,), (1,)), ((), ())), preferred_element_type=jnp.float32),
    )
    step = 512
    for start in range(0, width, step):
        columns = slice(start, start + step)
        store(
            columns, jnp.dot(pick, latents_ref[:, columns], preferred_element_type=jnp.float32)
        )


def pack(me, target, latents, group_count, seq_count, capacity):
    width = latents.shape[1] + LANES
    whole = pl.BlockSpec(memory_space=pltpu.VMEM)
    return pl.pallas_call(
        functools.partial(pack_kernel, seq_count=seq_count),
        in_specs=[pl.BlockSpec(memory_space=pltpu.SMEM), whole, whole],
        out_specs=[whole] * group_count,
        out_shape=[jax.ShapeDtypeStruct((capacity, width), jnp.bfloat16)] * group_count,
        compiler_params=params(24),
        cost_estimate=cost(
            2 * group_count * capacity * latents.size, 2 * width * (group_count * capacity + latents.shape[0])
        ),
        name="pack",
    )(me, target[None, :], latents)


def join_kernel(*refs):
    out_ref = refs[-1]
    start = 0
    for ref in refs[:-1]:
        out_ref[:, start : start + ref.shape[1]] = ref[...]
        start += ref.shape[1]


def join(arrays):
    rows = arrays[0].shape[0]
    columns = sum(array.shape[1] for array in arrays)
    whole = pl.BlockSpec(memory_space=pltpu.VMEM)
    return pl.pallas_call(
        join_kernel,
        in_specs=[whole] * len(arrays),
        out_specs=whole,
        out_shape=jax.ShapeDtypeStruct((rows, columns), arrays[0].dtype),
        compiler_params=params(8),
        cost_estimate=cost(0, 0),
        name="join",
    )(*arrays)


def marks_kernel(me_ref, *refs, per_block):
    segment_refs, (meta_ref, other_ref, clip_ref) = refs[:-3], refs[-3:]
    tiles = len(segment_refs) * per_block
    every = jnp.concatenate([ref[...] for ref in segment_refs], axis=0)
    lines = lax.broadcasted_iota(jnp.int32, (16, TILE), 0)
    lanes = lax.broadcasted_iota(jnp.int32, (16, LANES), 1)
    unit = one_hot(lax.broadcasted_iota(jnp.int32, (16, LANES), 0) == lanes)
    for tile in range(tiles):
        relative, chunk = tile // per_block, tile % per_block
        mine = segment_refs[relative][:, chunk * TILE : (chunk + 1) * TILE]
        meta_ref[tile] = jnp.sum((every < jnp.min(mine)).astype(jnp.int32))
        meta_ref[tiles + tile] = jnp.sum((every <= jnp.max(mine)).astype(jnp.int32))
        hit = lax.dot_general(
            one_hot(lines == mine), unit, (((0,), (0,)), ((), ())), preferred_element_type=jnp.float32
        )
        used = lax.broadcasted_iota(jnp.int32, (TILE, LANES), 1) < 16
        other_ref[tile] = jnp.where(used & (hit < 0.5), BLOCKED, 0.0).astype(jnp.bfloat16)
        place = lax.bitwise_xor(me_ref[0], relative) * per_block + chunk
        clip_ref[pl.ds(pl.multiple_of(place * TILE, TILE), TILE), :] = hit.astype(jnp.bfloat16)


def marks(me, segments, per_block):
    whole = pl.BlockSpec(memory_space=pltpu.VMEM)
    scalars = pl.BlockSpec(memory_space=pltpu.SMEM)
    tiles = len(segments) * per_block
    return pl.pallas_call(
        functools.partial(marks_kernel, per_block=per_block),
        in_specs=[scalars] + [whole] * len(segments),
        out_specs=[scalars, whole, whole],
        out_shape=[
            jax.ShapeDtypeStruct((2 * tiles,), jnp.int32),
            jax.ShapeDtypeStruct((tiles, TILE, LANES), jnp.bfloat16),
            jax.ShapeDtypeStruct((tiles * TILE, LANES), jnp.bfloat16),
        ],
        compiler_params=params(8),
        cost_estimate=cost(0, 0),
        name="marks",
    )(me, *segments)


def place_kernel(clip_bucket_ref, segment_ref, table_ref, *refs, start):
    incoming_refs, refs = refs[:-5], refs[-5:]
    out_ref, *half_refs, held_ref, sems = refs
    tile, width = out_ref.shape
    slots = held_ref.shape[0]
    capacity = incoming_refs[0].shape[0]
    buckets = table_ref.shape[0]

    @pl.when(pl.program_id(0) == 0)
    def _():
        copies = [
            pltpu.make_async_copy(ref, held_ref.at[pl.ds(i * capacity, capacity)], sems.at[i])
            for i, ref in enumerate(incoming_refs)
        ]
        for copy in copies:
            copy.start()
        for copy in copies:
            copy.wait()

    lines = lax.broadcasted_iota(jnp.int32, (16, LANES), 0)
    lanes = lax.broadcasted_iota(jnp.int32, (16, LANES), 1)
    reader = jnp.where(lines == 0, jnp.where(lanes == 0, 16, jnp.where(lanes == 1, 1, 0)), 0)
    reader = jnp.where((lines == 1) & (lanes == 2), 1, reader)
    found = lax.dot_general(
        reader.astype(jnp.float32).astype(jnp.bfloat16),
        held_ref[:, width:],
        (((1,), (1,)), ((), ())),
        preferred_element_type=jnp.float32,
    ).astype(jnp.int32)
    rows = jnp.where(found[1:2] > 0, found[0:1], -1)
    first = pl.program_id(0) * tile + start
    mine = lax.broadcasted_iota(jnp.int32, (tile, slots), 0) + first
    pick = one_hot(mine == rows)
    placed = jnp.dot(pick, held_ref[:, :width], preferred_element_type=jnp.float32)
    row_mean = jnp.mean(placed, axis=1, keepdims=True)
    centered = placed - row_mean
    row_var = jnp.mean(centered * centered, axis=1, keepdims=True)
    normalized = centered * lax.rsqrt(row_var + 1e-06)
    lines = lax.broadcasted_iota(jnp.int32, (16, buckets), 0)
    bucket_of = jnp.full((16, buckets), -1, jnp.int32)
    for clip in range(clip_bucket_ref.shape[1]):
        bucket_of = jnp.where(lines == clip, clip_bucket_ref[0, clip], bucket_of)
    clip_hit = lax.broadcasted_iota(jnp.int32, (16, tile), 0) == segment_ref[...]
    bucket_hit = lax.dot_general(
        one_hot(clip_hit),
        one_hot(bucket_of == lax.broadcasted_iota(jnp.int32, (16, buckets), 1)),
        (((0,), (0,)), ((), ())),
        preferred_element_type=jnp.float32,
    ).astype(jnp.bfloat16)
    shift = jnp.dot(bucket_hit, table_ref[:, :width], preferred_element_type=jnp.float32)
    scale = jnp.dot(bucket_hit, table_ref[:, width:], preferred_element_type=jnp.float32)
    result = (normalized * (1.0 + scale) + shift).astype(jnp.bfloat16)
    out_ref[...] = result
    for which, half_ref in enumerate(half_refs):

        @pl.when(pl.program_id(0) == which)
        def _():
            half_ref[...] = result


def place_and_norm(clip_bucket, segments, incoming, mod_table, start, tile):
    capacity, wide = incoming[0].shape
    width = wide - LANES
    slots = capacity * len(incoming)
    first = start // tile
    return pl.pallas_call(
        functools.partial(place_kernel, start=start),
        grid=(2,),
        in_specs=[
            pl.BlockSpec(memory_space=pltpu.SMEM),
            pl.BlockSpec((1, tile), lambda i: (0, i + first)),
            pl.BlockSpec(mod_table.shape, lambda i: (0, 0)),
        ]
        + [pl.BlockSpec(memory_space=pl.ANY)] * len(incoming),
        out_specs=[pl.BlockSpec((tile, width), lambda i: (i, 0))]
        + [pl.BlockSpec((tile, width), lambda i: (0, 0))] * 2,
        out_shape=[jax.ShapeDtypeStruct((2 * tile, width), jnp.bfloat16)]
        + [jax.ShapeDtypeStruct((tile, width), jnp.bfloat16)] * 2,
        scratch_shapes=[
            pltpu.VMEM((slots, wide), jnp.bfloat16),
            pltpu.SemaphoreType.DMA((len(incoming),)),
        ],
        compiler_params=params(20),
        cost_estimate=cost(0, 0),
        name="place_and_norm",
    )(clip_bucket, segments, mod_table, *incoming)


def attend_tile(first, last, query, other, key_ref, value_ref, clip_ref, write):
    length = key_ref.shape[0]
    tile, columns = query.shape
    heads = columns // HEAD_DIM
    factor = (HEAD_DIM ** (-0.5)) * 1.4426950408889634
    reach = min(length, (tile - 1 + 2 * (MOST - 1) + 2 * LANES - 1) // LANES * LANES)
    sizes = [size for size in (512, 768, 1024) if size < reach] + [reach]
    first = first // LANES * LANES
    need = last - first

    def work(size):
        start = pl.multiple_of(jnp.clip(first, 0, length - size), LANES)
        clip = clip_ref[pl.ds(start, size), :]

        def score(head):
            lanes = slice(head * HEAD_DIM, (head + 1) * HEAD_DIM)
            return lax.dot_general(
                jnp.concatenate([key_ref[pl.ds(start, size), lanes], clip], axis=1),
                jnp.concatenate([query[:, lanes], other], axis=1),
                (((1,), (1,)), ((), ())),
                preferred_element_type=jnp.float32,
            )

        def finish(head, scores):
            lanes = slice(head * HEAD_DIM, (head + 1) * HEAD_DIM)
            top = jnp.max(scores, axis=0, keepdims=True)
            weights = jnp.exp2((scores - top) * factor)
            total = jnp.sum(weights, axis=0, keepdims=True)
            mixed = jnp.dot(
                value_ref[lanes, pl.ds(start, size)],
                weights.astype(jnp.bfloat16),
                preferred_element_type=jnp.float32,
            )
            write(lanes, (mixed / total).T.astype(jnp.bfloat16))

        scores = score(0)
        for head in range(heads):
            following = score(head + 1) if head + 1 < heads else None
            finish(head, scores)
            scores = following

    least = 0
    for size in sizes:

        @pl.when((need > least) & (need <= size))
        def _():
            work(size)

        least = size


def load_parts(part_refs, part_rows, hidden, sems, block):
    copies, start = [], 0
    for count, ref in zip(part_rows, part_refs):
        spot = hidden.at[pl.ds(start, count)]
        copies.append(pltpu.make_async_copy(ref, spot, sems.at[start // block]))
        start += count
    return copies


def arrived(hidden, sems, group, block):
    spot = pl.ds(pl.multiple_of(group * block, block), block)
    pltpu.make_async_copy(hidden.at[spot], hidden.at[spot], sems.at[group]).wait()
    return hidden.at[spot]


def halves(me_ref, half, depth):
    near_start = pl.multiple_of(me_ref[0] // half * depth, depth)
    return near_start, pl.multiple_of(depth - near_start, depth)


def near_half_kernel(me_ref, *refs, part_count):
    part_refs, refs = refs[:part_count], refs[part_count:]
    piece_refs, (weights, total, hidden, hidden_sems, weight_sems) = refs[:-5], refs[-5:]
    rows = piece_refs[0].shape[0]
    half = len(piece_refs)
    near_start, _ = halves(me_ref, half, half * rows)
    copies = []
    for relative, ref in enumerate(piece_refs):
        place = lax.bitwise_xor(me_ref[0], relative) % half * rows
        spot = weights.at[pl.ds(pl.multiple_of(place, rows), rows)]
        copies.append(pltpu.make_async_copy(ref, spot, weight_sems.at[relative]))
    count = part_refs[0].shape[0]
    for i, ref in enumerate(part_refs):
        spot = hidden.at[pl.ds(i * count, count)]
        source = ref.at[:, pl.ds(near_start, half * rows)]
        copies.append(pltpu.make_async_copy(source, spot, hidden_sems.at[i]))
    for copy in copies:
        copy.start()
    for copy in copies:
        copy.wait()
    total[...] = jnp.dot(hidden[...], weights[...], preferred_element_type=jnp.float32)


def near_half(me, parts, pieces):
    rows, all_columns = pieces[0].shape
    depth = rows * len(pieces)
    block = sum(part.shape[0] for part in parts)
    anywhere = pl.BlockSpec(memory_space=pl.ANY)
    whole = pl.BlockSpec(memory_space=pltpu.VMEM)
    return pl.pallas_call(
        functools.partial(near_half_kernel, part_count=len(parts)),
        in_specs=[pl.BlockSpec(memory_space=pltpu.SMEM)] + [anywhere] * (len(parts) + len(pieces)),
        out_specs=[whole] * 2,
        out_shape=[
            jax.ShapeDtypeStruct((depth, all_columns), jnp.bfloat16),
            jax.ShapeDtypeStruct((block, all_columns), jnp.float32),
        ],
        scratch_shapes=[
            pltpu.VMEM((block, depth), jnp.bfloat16),
            pltpu.SemaphoreType.DMA((len(parts),)),
            pltpu.SemaphoreType.DMA((len(pieces),)),
        ],
        compiler_params=params(16),
        cost_estimate=cost(2 * block * depth * all_columns, 0),
        name="near_half",
    )(me, *parts, *pieces)


def first_kernel(me_ref, near_weights, begun, *refs, own_count, part_rows, per_block):
    own_refs, refs = refs[:own_count], refs[own_count:]
    part_refs, refs = refs[: len(part_rows)], refs[len(part_rows) :]
    piece_refs, refs = refs[:-8], refs[-8:]
    weights, queries, keys, values, own, hidden, part_sems, weight_sems = refs
    rows = piece_refs[0].shape[0]
    columns = keys.shape[2]
    half = len(piece_refs)
    depth = half * rows
    near_start, far_start = halves(me_ref, half, depth)
    pieces = []
    for i, ref in enumerate(piece_refs):
        place = lax.bitwise_xor(me_ref[0], half + i) % half * rows
        spot = weights.at[pl.ds(pl.multiple_of(place, rows), rows)]
        pieces.append(pltpu.make_async_copy(ref, spot, weight_sems.at[i]))
    block = per_block * TILE
    parts = load_parts(part_refs, part_rows, hidden, part_sems, block)
    count = own_refs[0].shape[0]
    owns = []
    for i, ref in enumerate(own_refs):
        spot = own.at[pl.ds(i * count, count)]
        source = ref.at[:, pl.ds(far_start, depth)]
        owns.append(pltpu.make_async_copy(source, spot, part_sems.at[1 + i]))
    for copy in parts + pieces + owns:
        copy.start()

    def store(group, whole):
        keys[group] = whole[:, columns : 2 * columns].astype(jnp.bfloat16)
        values[group] = whole[:, 2 * columns :].T.astype(jnp.bfloat16)
        for i in range(per_block):
            queries[group * per_block + i] = whole[i * TILE : (i + 1) * TILE, :columns].astype(
                jnp.bfloat16
            )

    mine = arrived(hidden, part_sems, 0, block)
    total = jnp.dot(
        mine[:, pl.ds(near_start, depth)], near_weights[...], preferred_element_type=jnp.float32
    )
    for copy in pieces:
        copy.wait()
    total += jnp.dot(
        mine[:, pl.ds(far_start, depth)], weights[...], preferred_element_type=jnp.float32
    )
    store(1, total)
    for copy in owns:
        copy.wait()
    store(0, begun[...] + jnp.dot(own[...], weights[...], preferred_element_type=jnp.float32))


def project_first(me, near_weights, begun, own_parts, parts, pieces, per_block):
    width = parts[0].shape[1]
    rows, all_columns = pieces[0].shape
    depth = rows * len(pieces)
    columns = all_columns // 3
    block = per_block * TILE
    anywhere = pl.BlockSpec(memory_space=pl.ANY)
    whole = pl.BlockSpec(memory_space=pltpu.VMEM)
    return pl.pallas_call(
        functools.partial(
            first_kernel,
            own_count=len(own_parts),
            part_rows=[part.shape[0] for part in parts],
            per_block=per_block,
        ),
        in_specs=[pl.BlockSpec(memory_space=pltpu.SMEM), whole, whole]
        + [anywhere] * (len(own_parts) + len(parts) + len(pieces)),
        out_specs=[whole] * 4,
        out_shape=[
            jax.ShapeDtypeStruct((depth, all_columns), jnp.bfloat16),
            jax.ShapeDtypeStruct((2 * per_block, TILE, columns), jnp.bfloat16),
            jax.ShapeDtypeStruct((2, block, columns), jnp.bfloat16),
            jax.ShapeDtypeStruct((2, columns, block), jnp.bfloat16),
        ],
        scratch_shapes=[
            pltpu.VMEM((block, depth), jnp.bfloat16),
            pltpu.VMEM((block, width), jnp.bfloat16),
            pltpu.SemaphoreType.DMA((1 + len(own_parts),)),
            pltpu.SemaphoreType.DMA((len(pieces),)),
        ],
        compiler_params=params(22),
        cost_estimate=cost(4 * block * width * all_columns, 0),
        name="project_first",
    )(me, near_weights, begun, *own_parts, *parts, *pieces)


def project_kernel(
    me_ref,
    meta_ref,
    other_ref,
    clip_ref,
    near_weights,
    far_weights,
    first_queries,
    first_keys,
    first_values,
    *refs,
    part_rows,
    group_count,
    seq_count,
    per_block,
):
    side = seq_count // 2
    far_tiles = side * per_block
    part_refs, refs = refs[: len(part_rows)], refs[len(part_rows) :]
    far_refs, refs = refs[:side], refs[side:]
    queries, keys, values, hidden, far, hidden_sems, copy_sems = refs
    me_seq = me_ref[1]
    columns = keys.shape[1]
    depth = near_weights.shape[0]
    near_start, far_start = halves(me_ref, group_count // 2, depth)
    block = per_block * TILE
    tiles = seq_count * per_block
    parts = load_parts(part_refs, part_rows, hidden, hidden_sems, block)
    moves = []
    for group in range(side):
        place = pl.multiple_of(lax.bitwise_xor(me_seq, 2 * group) * block, block)
        moves += [
            (first_keys.at[group], keys.at[pl.ds(place, block)]),
            (first_values.at[group], values.at[:, pl.ds(place, block)]),
            (
                first_queries.at[pl.ds(group * per_block, per_block)],
                queries.at[pl.ds(2 * group * per_block, per_block)],
            ),
        ]
    moves = [
        pltpu.make_async_copy(source, place, copy_sems.at[i])
        for i, (source, place) in enumerate(moves)
    ]
    for copy in parts + moves:
        copy.start()

    def step(group, _):
        mine = arrived(hidden, hidden_sems, group, block)
        whole = jnp.dot(
            mine[:, pl.ds(near_start, depth)], near_weights[...], preferred_element_type=jnp.float32
        ) + jnp.dot(
            mine[:, pl.ds(far_start, depth)], far_weights[...], preferred_element_type=jnp.float32
        )
        relative = 2 * group + 1
        place = pl.multiple_of(lax.bitwise_xor(me_seq, relative) * block, block)
        keys[pl.ds(place, block), :] = whole[:, columns : 2 * columns].astype(jnp.bfloat16)
        values[:, pl.ds(place, block)] = whole[:, 2 * columns :].T.astype(jnp.bfloat16)
        for i in range(per_block):
            queries[relative * per_block + i] = whole[i * TILE : (i + 1) * TILE, :columns].astype(
                jnp.bfloat16
            )
        return 0

    lax.fori_loop(0, side, step, 0)
    for copy in moves:
        copy.wait()

    def far_step(i, _):
        tile = tiles - far_tiles + i

        def write(lanes, result):
            far[i, :, lanes] = result

        attend_tile(
            meta_ref[tile],
            meta_ref[tiles + tile],
            queries.at[tile],
            other_ref[tile],
            keys,
            values,
            clip_ref,
            write,
        )
        return 0

    lax.fori_loop(0, far_tiles, far_step, 0)
    for i, far_ref in enumerate(far_refs):
        for j in range(per_block):
            far_ref[j * TILE : (j + 1) * TILE, :] = far[i * per_block + j]


def project_and_attend(me, meta, other, clip, parts, first, group_count, seq_count, per_block):
    depth, all_columns = first[0].shape
    width = 2 * depth
    columns = all_columns // 3
    side = seq_count // 2
    tiles = seq_count * per_block
    length = tiles * TILE
    whole = pl.BlockSpec(memory_space=pltpu.VMEM)
    scalars = pl.BlockSpec(memory_space=pltpu.SMEM)
    return pl.pallas_call(
        functools.partial(
            project_kernel,
            part_rows=[part.shape[0] for part in parts],
            group_count=group_count,
            seq_count=seq_count,
            per_block=per_block,
        ),
        in_specs=[scalars, scalars]
        + [whole] * (2 + len(first))
        + [pl.BlockSpec(memory_space=pl.ANY)] * len(parts),
        out_specs=[whole] * (side + 3),
        out_shape=[jax.ShapeDtypeStruct((per_block * TILE, columns), jnp.bfloat16)] * side
        + [
            jax.ShapeDtypeStruct((tiles, TILE, columns), jnp.bfloat16),
            jax.ShapeDtypeStruct((length, columns), jnp.bfloat16),
            jax.ShapeDtypeStruct((columns, length), jnp.bfloat16),
        ],
        scratch_shapes=[
            pltpu.VMEM((length // 2, width), jnp.bfloat16),
            pltpu.VMEM((side * per_block, TILE, columns), jnp.bfloat16),
            pltpu.SemaphoreType.DMA((side,)),
            pltpu.SemaphoreType.DMA((3 * side,)),
        ],
        compiler_params=params(22),
        cost_estimate=cost(2 * length * width * all_columns, 0),
        name="project_and_attend",
    )(me, meta, other, clip, *first, *parts)


def near_kernel(meta_ref, other_ref, query_ref, key_ref, value_ref, clip_ref, *refs):
    out_refs, result_ref = refs[:-1], refs[-1]
    index = pl.program_id(0)
    tiles = meta_ref.shape[0] // 2

    def write(lanes, result):
        result_ref[:, lanes] = result

    attend_tile(
        meta_ref[index],
        meta_ref[tiles + index],
        query_ref.at[0],
        other_ref[0],
        key_ref,
        value_ref,
        clip_ref,
        write,
    )
    for which, out_ref in enumerate(out_refs):

        @pl.when(index == which)
        def _():
            out_ref[...] = result_ref[...]


def attend_near(meta, other, query, keys, values, clip, tiles):
    _, tile, columns = query.shape

    def whole(array):
        return pl.BlockSpec(array.shape, lambda i, meta: (0, 0))

    return pl.pallas_call(
        near_kernel,
        grid_spec=pltpu.PrefetchScalarGridSpec(
            num_scalar_prefetch=1,
            grid=(tiles,),
            in_specs=[
                pl.BlockSpec((1, tile, LANES), lambda i, meta: (i, 0, 0)),
                pl.BlockSpec((1, tile, columns), lambda i, meta: (i, 0, 0)),
                whole(keys),
                whole(values),
                whole(clip),
            ],
            out_specs=[pl.BlockSpec((tile, columns), lambda i, meta: (0, 0))] * tiles,
            scratch_shapes=[pltpu.VMEM((tile, columns), jnp.bfloat16)],
        ),
        out_shape=[jax.ShapeDtypeStruct((tile, columns), jnp.bfloat16)] * tiles,
        compiler_params=params(20),
        cost_estimate=cost(8 * query.size * keys.shape[0], 6 * keys.size),
        name="attend_near",
    )(meta, other, query, keys, values, clip)


def order_kernel(me_ref, *refs, counts):
    part_refs, out_ref = refs[:-1], refs[-1]
    column = pl.program_id(0)
    for relative, count in enumerate(counts):
        mine, part_refs = part_refs[:count], part_refs[count:]

        @pl.when(lax.bitwise_xor(column, me_ref[0]) == relative)
        def _():
            start = 0
            for part in mine:
                out_ref[start : start + part.shape[0], :] = part[...]
                start += part.shape[0]


def side_by_side(me, parts):
    rows = sum(part.shape[0] for part in parts[0])
    columns = parts[0][0].shape[1]
    flat = [part for group in parts for part in group]
    return pl.pallas_call(
        functools.partial(order_kernel, counts=[len(group) for group in parts]),
        grid_spec=pltpu.PrefetchScalarGridSpec(
            num_scalar_prefetch=1,
            grid=(len(parts),),
            in_specs=[pl.BlockSpec(part.shape, lambda i, me: (0, 0)) for part in flat],
            out_specs=pl.BlockSpec((rows, columns), lambda i, me: (0, i)),
        ),
        out_shape=jax.ShapeDtypeStruct((rows, columns * len(parts)), jnp.bfloat16),
        compiler_params=params(12),
        cost_estimate=cost(0, 4 * rows * columns * len(parts)),
        name="side_by_side",
    )(me, *flat)


def swap(value, axis, distance):
    count = lax.axis_size(axis)
    return lax.ppermute(value, axis, [(i, i ^ distance) for i in range(count)])


def swap_gather(blocks, axis, distance):
    blocks = dict(blocks)
    while distance:
        for relative in sorted(blocks):
            blocks[relative ^ distance] = swap(blocks[relative], axis, distance)
        distance //= 2
    return blocks


def after(value, *others):
    return lax.optimization_barrier((value, *others))[0]


def on_device(latents, target, segment_ids, clip_bucket, mod_table, w_query, w_key, w_value):
    local_rows = latents.shape[0]
    group_count = lax.axis_size("dp")
    seq_count = lax.axis_size("seq")
    capacity = (max(2, 3 * local_rows // (2 * group_count)) + 15) // 16 * 16
    per_block = local_rows // TILE
    side = seq_count // 2
    half = group_count // 2
    me_dp = lax.axis_index("dp").astype(jnp.int32)[None]
    me_seq = lax.axis_index("seq").astype(jnp.int32)[None]
    single = [1 << i for i in reversed(range(half.bit_length() - 1))]
    several = [r for r in range(1, half) if r not in single]

    packed = pack(me_dp, target, latents, group_count, seq_count, capacity)
    incoming = [packed[0]]
    for r in range(1, group_count):
        incoming.append(swap(packed[r], "dp", r))
    order = [r for pair in zip(reversed(range(half, group_count)), reversed(range(half))) for r in pair]
    begun = [incoming[half - 1]]
    own = join([after(w_query, *begun), w_key, w_value])
    pieces = {0: own}

    def piece(r, *ahead):
        bit = r & -r
        return swap(after(pieces[r ^ bit], *ahead), "dp", bit)

    for r in single:
        pieces[r] = piece(r)
    segments = [segment_ids]
    for r in range(1, seq_count):
        segments.append(swap(after(segment_ids, incoming[half + 1]), "seq", r))
    meta, other, clip = marks(me_seq, segments, per_block)
    done = [pieces[r] for r in single] + [meta] + [incoming[r] for r in order]

    pieces[half] = swap(after(own, *done), "dp", half)
    for r in several:
        pieces[r] = piece(r, *done)
    ready = after(segment_ids, *done)
    quarter = local_rows // 4
    blocks = {}
    for pair in range(2):
        whole, *quarters = place_and_norm(
            clip_bucket, ready, [incoming[r] for r in order], mod_table, 2 * pair * quarter, quarter
        )
        blocks[0, "pair", pair] = whole
        for which, block in enumerate(quarters):
            blocks[0, "quarter", 2 * pair + which] = block

    def spread(relative, kind, part, distance, *ahead):
        moved = swap(after(blocks[relative, kind, part], *ahead), "seq", distance)
        blocks[relative ^ distance, kind, part] = moved
        return moved

    done = [
        pieces[half],
        spread(0, "quarter", 0, side),
        spread(0, "quarter", 1, side),
        blocks[0, "pair", 1],
        *[pieces[r] for r in several],
    ]
    for r in single:
        pieces[half ^ r] = piece(half ^ r, *done)
    for r in several:
        pieces[half ^ r] = piece(half ^ r, *[pieces[half ^ other] for other in single])
    me = jnp.concatenate([me_dp, me_seq])
    own_parts = [blocks[0, "pair", part] for part in range(2)]
    near_weights, begun = near_half(me, own_parts, [pieces[r] for r in range(half)])
    third = spread(0, "quarter", 2, side, *done)
    spread(0, "quarter", 3, side, *done)
    for part in range(2):
        spread(0, "pair", part, 1, third, near_weights)
    for part in range(4):
        spread(side, "quarter", part, 1, third, near_weights)

    def parts(r):
        kind, count = ("pair", 2) if r < side else ("quarter", 4)
        return [blocks[r, kind, part] for part in range(count)]

    first = project_first(
        me,
        near_weights,
        begun,
        own_parts,
        parts(side),
        [pieces[r] for r in range(half, group_count)],
        per_block,
    )
    *far, query, keys, values = project_and_attend(
        me,
        meta,
        other,
        clip,
        [part for r in range(1, seq_count, 2) for part in parts(r)],
        [near_weights, *first],
        group_count,
        seq_count,
        per_block,
    )
    near = attend_near(meta, other, query, keys, values, clip, side * per_block)
    outs = [near[r * per_block : (r + 1) * per_block] for r in range(side)]
    outs += [[block] for block in far]
    outs = [[swap(out, "seq", r) if r else out for out in group] for r, group in enumerate(outs)]
    return side_by_side(me_seq, outs)


def solution(mesh):
    in_specs = (
        P(("dp", "seq"), None),
        P(("dp", "seq")),
        P("dp", "seq"),
        P("dp", None),
        P(),
        P("dp", "seq"),
        P("dp", "seq"),
        P("dp", "seq"),
    )
    out_specs = P(("dp", "seq"), None)
    return jax.shard_map(
        on_device, mesh=mesh, in_specs=in_specs, out_specs=out_specs, check_vma=False
    )
```

time: 741 us -> 257 us (0.35)
  waiting for transfers between devices: 484 us -> 139 us
  matrix products: 107 us -> 0 us
  Pallas kernels: 0 us -> 59.9 us
  blocking collectives: 44.8 us -> 0 us
  local copies, waits for them, and re-layouts: 45.8 us -> 2.59 us
  starting transfers between devices: 23.6 us -> 54.4 us
  between operations: 14.1 us -> 0.16 us
  other arithmetic: 13.7 us -> 0.07 us
    all_gather x6 -> x0, waiting for transfers between devices: 299 us -> none  [the longest x1 124 us: on_device(): lax.all_gather(columns_full[0], 'dp', axis=0, tiled=True)]
    all_to_all x5 -> x0, waiting for transfers between devices: 183 us -> none  [the longest x1 183 us: on_device(): lax.all_to_all(outgoing, 'dp', split_axis=0, concat_axis=0, tiled=True)]
    ppermute x0 -> x31, waiting for transfers between devices: none -> 139 us  [swap(): return lax.ppermute(value, axis, [(i, i ^ distance) for i in range(count)])]
    dot_general x8 -> x0, matrix products: 65.7 us -> none  [the longest x4 29.1 us: attend_block(): jnp.einsum('hqk,khd->qhd', weights_bf, value_heads, preferred_element_typ...]
    pallas_call x0 -> x10, Pallas kernels: none -> 59.9 us  [the longest x1 15.9 us: project_and_attend(): pl.pallas_call(functools.partial(project_kernel, part_rows=[part.shape[0]...]
    ppermute x0 -> x31, starting transfers between devices: none -> 54.4 us  [swap(): return lax.ppermute(value, axis, [(i, i ^ distance) for i in range(count)])]
    sub x4 -> x0, matrix products: 41.7 us -> none  [attend_block(): exponent = jnp.exp(scores - row_max)]
    all_to_all x1 -> x0, blocking collectives: 23.7 us -> none  [on_device(): lax.all_to_all(head_output, 'seq', split_axis=0, concat_axis=1, tiled=True)]
  transfers between devices with their start and end apart: 11 -> 31, of which waited for: 6 -> 15; matrix products, arithmetic and copies ran while one was open for 12% -> 0% of each run, Pallas kernels for 0% -> 15%
where the time goes in v1:
time: 257 us; the launch traced here: 256 us
  waiting for transfers between devices  139 us (54%)
  Pallas kernels  59.9 us (23%)
  starting transfers between devices  54.4 us (21%)
  local copies, waits for them, and re-layouts  2.59 us (1%)
    ppermute x31, waiting for transfers between devices, swap(): return lax.ppermute(value, axis, [(i, i ^ distance) for i in range(count)])  139 us
    ppermute x31, starting transfers between devices, swap(): return lax.ppermute(value, axis, [(i, i ^ distance) for i in range(count)])  54.4 us
    pallas_call x1, Pallas kernels, project_and_attend(): pl.pallas_call(functools.partial(project_kernel, part_rows=[part.shape[0]...  15.9 us
    pallas_call x2, Pallas kernels, place_and_norm(): pl.pallas_call(functools.partial(place_kernel, start=start), grid=(2,), i...  12.1 us
    pallas_call x1, Pallas kernels, project_first(): pl.pallas_call(functools.partial(first_kernel, own_count=len(own_parts),...  10.3 us
    pallas_call x1, Pallas kernels, attend_near(): pl.pallas_call(near_kernel, grid_spec=pltpu.PrefetchScalarGridSpec(num_sc...  7.35 us
  transfers between devices with their start and end apart: 31, of which 15 were waited for; matrix products, arithmetic and copies ran while one was open for 0% of the time, Pallas kernels for 15%

profile of v1, /device:TPU:0, one launch (start us, length us, event | category | flops | bytes accessed | tf_op | source)
XLA Modules:
  0.0 256.4 jit_solution(15539402643652826051)
XLA Ops:
  0.0 1.9 copy-done.6
  1.9 0.7 copy-done.7
  2.6 4.2 %pack.1 = (bf16[96,3200]{1,0:T(8,128)(2,1)S(1)}, bf16[96,3200]{1,0:T(8,128)(2,1)}, bf16[96,3200]{1,0:T(8,128)(2,1)}, bf16[96,3200]{1,0:T(8,128)(2,1)S(1)}, bf16[...) custom-call(s32[1]{0:T(128)} %bitcast.1.me_ref, ...), custom_call_target="tpu_custom_call" | custom-call | flops 2415919104 | bytes 8192000 | tf_op jit(solution)/shard_map/pack/pallas_call | solution.py:71
  6.8 4.0 %collective-permute-start.4 = (bf16[96,3200]{1,0:T(8,128)(2,1)S(1)}, bf16[96,3200]{1,0:T(8,128)(2,1)S(1)}, u32[]{:S(2)}, u32[]{:S(2)}) collective-permute-start(bf16[96,3200]{1,0:T(8,128)(2,1)S(1)} %get-tuple-element.57), channel_id=1, source_target_pairs={{0,12},{4,8},{8,4},{12,0},{16,28},{20,24},{24,20},{28,16},{1,13},{... | collective-permute-start | bytes 1843208 | tf_op jit(solution)/shard_map/ppermute | solution.py:657
  10.7 2.5 collective-permute-start
  13.3 1.2 collective-permute-start.7
  14.5 3.6 %collective-permute-start.8 = (bf16[96,3200]{1,0:T(8,128)(2,1)S(1)}, bf16[96,3200]{1,0:T(8,128)(2,1)S(1)}, u32[]{:S(2)}, u32[]{:S(2)}) collective-permute-start(bf16[96,3200]{1,0:T(8,128)(2,1)S(1)} %get-tuple-element.60), channel_id=1, source_target_pairs={{0,24},{4,28},{8,16},{12,20},{16,8},{20,12},{24,0},{28,4},{1,25},{... | collective-permute-start | bytes 1843208 | tf_op jit(solution)/shard_map/ppermute | solution.py:657
  18.1 18.5 %collective-permute-done.4.refs_1_ = bf16[96,3200]{1,0:T(8,128)(2,1)S(1)} collective-permute-done((bf16[96,3200]{1,0:T(8,128)(2,1)S(1)}, bf16[96,3200]{1,0:T(8,128)(2,1)S(1)}, u32[]{:S(2)}, u32[]{:S(2)}) %collective-permute-start.4) | collective-permute-done | bytes 614432 | tf_op jit(solution)/shard_map/ppermute | solution.py:657
  36.5 1.0 join.1.refs_2_
  37.5 2.1 collective-permute-start.6
  39.7 29.2 %collective-permute-done.refs_4_ = bf16[96,3200]{1,0:T(8,128)(2,1)S(1)} collective-permute-done((bf16[96,3200]{1,0:T(8,128)(2,1)S(1)}, bf16[96,3200]{1,0:T(8,128)(2,1)S(1)}, u32[]{:S(2)}, u32[]{:S(2)}) %collective-permute-start) | collective-permute-done | bytes 614432 | tf_op jit(solution)/shard_map/ppermute | solution.py:657
  68.9 1.6 collective-permute-start.2
  70.5 0.3 collective-permute-start.1
  70.7 1.1 collective-permute-done.3.refs_3_
  71.9 21.5 %collective-permute-start.9 = (bf16[96,3200]{1,0:T(8,128)(2,1)}, bf16[96,3200]{1,0:T(8,128)(2,1)}, u32[]{:S(2)}, u32[]{:S(2)}) collective-permute-start(bf16[96,3200]{1,0:T(8,128)(2,1)} %get-tuple-element.61), channel_id=1, source_target_pairs={{0,8},{4,12},{8,0},{12,4},{16,24},{20,28},{24,16},{28,20},{1,9},{5... | collective-permute-start | bytes 1843208 | tf_op jit(solution)/shard_map/ppermute | solution.py:657
  93.4 1.5 collective-permute-start.10
  94.9 1.1 collective-permute-start.11
  96.0 2.8 %marks.1 = (s32[16]{0:T(128)S(1)}, bf16[8,256,128]{2,1,0:T(8,128)(2,1)S(1)}, bf16[2048,128]{1,0:T(8,128)(2,1)S(1)}) custom-call(s32[1]{0:T(128)} %bitcast.me_ref, s32[1,512]{1,0:T(1,128)S(1)} %copy-done.4, s32[1,512]{1,0:T(1,128)S(1)} %collective-permute-done.1.refs_1_, s32[1,512]{1,0:T(1,128)S(1)} %collective-permute-done.2.refs_2_, ...), custom_call_target="tpu_custom_call" | custom-call | tf_op jit(solution)/shard_map/marks/pallas_call | solution.py:132
  98.8 21.3 %collective-permute-done.9.refs_3_ = bf16[96,3200]{1,0:T(8,128)(2,1)} collective-permute-done((bf16[96,3200]{1,0:T(8,128)(2,1)}, bf16[96,3200]{1,0:T(8,128)(2,1)}, u32[]{:S(2)}, u32[]{:S(2)}) %collective-permute-start.9) | collective-permute-done | bytes 614432 | tf_op jit(solution)/shard_map/ppermute | solution.py:657
  120.1 4.9 %collective-permute-done.11.refs_6_ = bf16[96,3200]{1,0:T(8,128)(2,1)} collective-permute-done((bf16[96,3200]{1,0:T(8,128)(2,1)}, bf16[96,3200]{1,0:T(8,128)(2,1)}, u32[]{:S(2)}, u32[]{:S(2)}) %collective-permute-start.11) | collective-permute-done | bytes 614432 | tf_op jit(solution)/shard_map/ppermute | solution.py:657
  125.1 0.5 collective-permute-start.12
  125.7 6.1 %place_and_norm.2 = (bf16[256,3072]{1,0:T(8,128)(2,1)S(1)}, bf16[128,3072]{1,0:T(8,128)(2,1)S(1)}, bf16[128,3072]{1,0:T(8,128)(2,1)S(1)}) custom-call(s32[1,8]{1,0:T(1,128)S(1)} %copy-done.5, s32[1,512]{1,0:T(1,128)S(1)} %copy-done.4, bf16[16,6144]{1,0:T(8,128)(2,1)S(1)} %copy-done, bf16[96,3200]{1,0:T(8,128)(2,1)S(1)} %collective-permute-done.7.refs_0_, ...), custom_call_target="tpu_custom_call" | custom-call | tf_op jit(solution)/shard_map/place_and_norm/pallas_call | solution.py:212
  131.8 1.6 collective-permute-start.14
  133.4 0.5 collective-permute-start.13
  133.9 6.0 %place_and_norm.3 = (bf16[256,3072]{1,0:T(8,128)(2,1)S(1)}, bf16[128,3072]{1,0:T(8,128)(2,1)S(1)}, bf16[128,3072]{1,0:T(8,128)(2,1)S(1)}) custom-call(s32[1,8]{1,0:T(1,128)S(1)} %copy-done.5, s32[1,512]{1,0:T(1,128)S(1)} %copy-done.4, bf16[16,6144]{1,0:T(8,128)(2,1)S(1)} %copy-done, bf16[96,3200]{1,0:T(8,128)(2,1)S(1)} %collective-permute-done.7.refs_0_, ...), custom_call_target="tpu_custom_call" | custom-call | tf_op jit(solution)/shard_map/place_and_norm/pallas_call | solution.py:212
  139.9 12.4 %collective-permute-done.14.refs_3_ = bf16[128,3072]{1,0:T(8,128)(2,1)S(1)} collective-permute-done((bf16[128,3072]{1,0:T(8,128)(2,1)S(1)}, bf16[128,3072]{1,0:T(8,128)(2,1)S(1)}, u32[]{:S(2)}, u32[]{:S(2)}) %collective-permute-start.14) | collective-permute-done | bytes 786464 | tf_op jit(solution)/shard_map/ppermute | solution.py:657
  152.4 14.8 %collective-permute-done.13.refs_2_ = bf16[128,3072]{1,0:T(8,128)(2,1)S(1)} collective-permute-done((bf16[128,3072]{1,0:T(8,128)(2,1)S(1)}, bf16[128,3072]{1,0:T(8,128)(2,1)S(1)}, u32[]{:S(2)}, u32[]{:S(2)}) %collective-permute-start.13) | collective-permute-done | bytes 786464 | tf_op jit(solution)/shard_map/ppermute | solution.py:657
  167.2 2.5 collective-permute-start.19
  169.6 1.5 collective-permute-start.18
  171.1 1.5 collective-permute-start.16
  172.7 0.5 collective-permute-start.17
  173.2 13.9 %collective-permute-done.19.refs_8_ = bf16[384,1152]{1,0:T(8,128)(2,1)S(1)} collective-permute-done((bf16[384,1152]{1,0:T(8,128)(2,1)S(1)}, bf16[384,1152]{1,0:T(8,128)(2,1)S(1)}, u32[]{:S(2)}, u32[]{:S(2)}) %collective-permute-start.19) | collective-permute-done | bytes 884768 | tf_op jit(solution)/shard_map/ppermute | solution.py:657
  187.1 2.4 collective-permute-done.18.refs_7_
  189.5 1.5 collective-permute-start.20
  190.9 4.5 %near_half.1 = (bf16[1536,1152]{1,0:T(8,128)(2,1)S(1)}, f32[512,1152]{1,0:T(8,128)S(1)}) custom-call(s32[2]{0:T(128)S(1)} %pad_add_fusion.me_ref, bf16[256,3072]{1,0:T(8,128)(2,1)S(1)} %get-tuple-element.84.refs_0_, bf16[256,3072]{1,0:T(8,128)(2,1)S(1)} %get-tuple-element.85.refs_1_, bf16[384,1152]{1,0:T(8,128)(2,1)} %join.1.refs_2_, ...), custom_call_target="tpu_custom_call" | custom-call | flops 1811939328 | tf_op jit(solution)/shard_map/near_half/pallas_call | solution.py:335
  195.6 0.5 collective-permute-start.21
  196.1 8.4 %collective-permute-done.17.refs_5_ = bf16[128,3072]{1,0:T(8,128)(2,1)S(1)} collective-permute-done((bf16[128,3072]{1,0:T(8,128)(2,1)S(1)}, bf16[128,3072]{1,0:T(8,128)(2,1)S(1)}, u32[]{:S(2)}, u32[]{:S(2)}) %collective-permute-start.17) | collective-permute-done | bytes 786464 | tf_op jit(solution)/shard_map/ppermute | solution.py:657
  204.5 0.5 collective-permute-start.25
  205.0 2.5 collective-permute-done.20.refs_9_
  207.5 10.3 %project_first.1 = (bf16[1536,1152]{1,0:T(8,128)(2,1)S(1)}, bf16[4,256,384]{2,1,0:T(8,128)(2,1)S(1)}, bf16[2,512,384]{2,1,0:T(8,128)(2,1)S(1)}, bf16[2,384,512]{2,1,0:T(8,128)(2,1)S(1)}) custom-call(s32[2]{0:T(128)S(1)} %pad_add_fusion.me_ref, bf16[1536,1152]{1,0:T(8,128)(2,1)S(1)} %get-tuple-element.69.near_weights, ...), custom_call_target="tpu_custom_call" | custom-call | flops 7247757312 | tf_op jit(solution)/shard_map/project_first/pallas_call | solution.py:411
  217.9 15.9 %project_and_attend.1 = (bf16[512,384]{1,0:T(8,128)(2,1)S(1)}, bf16[512,384]{1,0:T(8,128)(2,1)S(1)}, bf16[8,256,384]{2,1,0:T(8,128)(2,1)S(1)}, bf16[2048,384]{1,0:T(8,128)(2,1)S(1)}, bf16[384,2048]{1,0:T(8,128)(2,1)S(1)}) custom-call(s32[2]{0:T(128)S(1)} %pad_add_fusion.me_ref, s32[16]{0:T(128)S(1)} %get-tuple-element.54.meta_ref, ...), custom_call_target="tpu_custom_call" | custom-call | flops 14495514624 | tf_op jit(solution)/shard_map/project_and_attend/pallas_call | solution.py:539
  233.7 2.9 %collective-permute-start.29 = (bf16[512,384]{1,0:T(8,128)(2,1)S(1)}, bf16[512,384]{1,0:T(8,128)(2,1)S(1)}, u32[]{:S(2)}, u32[]{:S(2)}) collective-permute-start(bf16[512,384]{1,0:T(8,128)(2,1)S(1)} %get-tuple-element.97), channel_id=1, source_target_pairs={{0,2},{1,3},{2,0},{3,1},{4,6},{5,7},{6,4},{7,5},{8,10},{9,11},{10,... | collective-permute-start | bytes 1179656 | tf_op jit(solution)/shard_map/ppermute | solution.py:657
  236.9 7.4 %attend_near.1 = (bf16[256,384]{1,0:T(8,128)(2,1)S(1)}, bf16[256,384]{1,0:T(8,128)(2,1)S(1)}, bf16[256,384]{1,0:T(8,128)(2,1)S(1)}, bf16[256,384]{1,0:T(8,128)(2,1)S(1)}) custom-call(s32[16]{0:T(128)S(1)} %get-tuple-element.54.meta_ref, bf16[8,256,128]{2,1,0:T(8,128)(2,1)S(1)} %get-tuple-element.55.other_ref, ...), custom_call_target="tpu_custom_call" | custom-call | flops 12884901888 | bytes 4718592 | tf_op jit(solution)/shard_map/attend_near/pallas_call | solution.py:600
  244.3 0.5 collective-permute-start.28
  244.8 0.9 collective-permute-done.27.refs_2_
  246.0 0.6 collective-permute-done.29.refs_4_
  246.6 8.1 %collective-permute-done.30.refs_5_ = bf16[512,384]{1,0:T(8,128)(2,1)S(1)} collective-permute-done((bf16[512,384]{1,0:T(8,128)(2,1)S(1)}, bf16[512,384]{1,0:T(8,128)(2,1)S(1)}, u32[]{:S(2)}, u32[]{:S(2)}) %collective-permute-start.30) | collective-permute-done | bytes 393248 | tf_op jit(solution)/shard_map/ppermute | solution.py:657
  254.7 1.7 side_by_side.1
  (41 shorter events, 1.0 us)
Async XLA Ops:
  0.0 1.9 copy-start.6
  1.9 0.7 copy-start.7
  2.6 33.9 %copy-start.1 = (bf16[384,384]{1,0:T(8,128)(2,1)S(1)}, bf16[384,384]{1,0:T(8,128)(2,1)}, u32[]{:S(2)}) copy-start(bf16[384,384]{1,0:T(8,128)(2,1)} %refs_0_.2) | copy-start | bytes 884740
  2.6 33.9 %copy-start.2 = (bf16[384,384]{1,0:T(8,128)(2,1)S(1)}, bf16[384,384]{1,0:T(8,128)(2,1)}, u32[]{:S(2)}) copy-start(bf16[384,384]{1,0:T(8,128)(2,1)} %refs_1_.1) | copy-start | bytes 884740
  2.6 33.9 %copy-start.3 = (bf16[384,384]{1,0:T(8,128)(2,1)S(1)}, bf16[384,384]{1,0:T(8,128)(2,1)}, u32[]{:S(2)}) copy-start(bf16[384,384]{1,0:T(8,128)(2,1)} %refs_2_.1) | copy-start | bytes 884740
  6.8 62.1 %copy-start.4 = (s32[1,512]{1,0:T(1,128)S(1)}, s32[1,512]{1,0:T(1,128)}, u32[]{:S(2)}) copy-start(s32[1,512]{1,0:T(1,128)} %segment_ref.1) | copy-start | bytes 6148
  6.8 118.9 %copy-start = (bf16[16,6144]{1,0:T(8,128)(2,1)S(1)}, bf16[16,6144]{1,0:T(8,128)(2,1)}, u32[]{:S(2)}) copy-start(bf16[16,6144]{1,0:T(8,128)(2,1)} %table_ref.3) | copy-start | bytes 589828
  6.8 118.9 %copy-start.5 = (s32[1,8]{1,0:T(1,128)S(1)}, s32[1,8]{1,0:T(1,128)}, u32[]{:S(2)}) copy-start(s32[1,8]{1,0:T(1,128)} %clip_bucket_ref.3) | copy-start | bytes 100
  6.8 29.7 %collective-permute-start.4 = (bf16[96,3200]{1,0:T(8,128)(2,1)S(1)}, bf16[96,3200]{1,0:T(8,128)(2,1)S(1)}, u32[]{:S(2)}, u32[]{:S(2)}) collective-permute-start(bf16[96,3200]{1,0:T(8,128)(2,1)S(1)} %get-tuple-element.57), channel_id=1, source_target_pairs={{0,12},{4,8},{8,4},{12,0},{16,28},{20,24},{24,20},{28,16},{1,13},{... | collective-permute-start | bytes 1843208 | tf_op jit(solution)/shard_map/ppermute | solution.py:657
  10.7 58.1 %collective-permute-start = (bf16[96,3200]{1,0:T(8,128)(2,1)S(1)}, bf16[96,3200]{1,0:T(8,128)(2,1)S(1)}, u32[]{:S(2)}, u32[]{:S(2)}) collective-permute-start(bf16[96,3200]{1,0:T(8,128)(2,1)S(1)} %get-tuple-element.52), channel_id=1, source_target_pairs={{0,20},{4,16},{8,28},{12,24},{16,4},{20,0},{24,12},{28,8},{1,21},{... | collective-permute-start | bytes 1843208 | tf_op jit(solution)/shard_map/ppermute | solution.py:657
  13.3 55.6 %collective-permute-start.7 = (bf16[96,3200]{1,0:T(8,128)(2,1)S(1)}, bf16[96,3200]{1,0:T(8,128)(2,1)S(1)}, u32[]{:S(2)}, u32[]{:S(2)}) collective-permute-start(bf16[96,3200]{1,0:T(8,128)(2,1)S(1)} %get-tuple-element.59), channel_id=1, source_target_pairs={{0,28},{4,24},{8,20},{12,16},{16,12},{20,8},{24,4},{28,0},{1,29},{... | collective-permute-start | bytes 1843208 | tf_op jit(solution)/shard_map/ppermute | solution.py:657
  14.5 56.0 %collective-permute-start.8 = (bf16[96,3200]{1,0:T(8,128)(2,1)S(1)}, bf16[96,3200]{1,0:T(8,128)(2,1)S(1)}, u32[]{:S(2)}, u32[]{:S(2)}) collective-permute-start(bf16[96,3200]{1,0:T(8,128)(2,1)S(1)} %get-tuple-element.60), channel_id=1, source_target_pairs={{0,24},{4,28},{8,16},{12,20},{16,8},{20,12},{24,0},{28,4},{1,25},{... | collective-permute-start | bytes 1843208 | tf_op jit(solution)/shard_map/ppermute | solution.py:657
  37.5 87.5 %collective-permute-start.6 = (bf16[384,1152]{1,0:T(8,128)(2,1)}, bf16[384,1152]{1,0:T(8,128)(2,1)}, u32[]{:S(2)}, u32[]{:S(2)}) collective-permute-start(bf16[384,1152]{1,0:T(8,128)(2,1)} %join.1.refs_2_), channel_id=1, source_target_pairs={{0,4},{4,0},{8,12},{12,8},{16,20},{20,16},{24,28},{28,24},{1,5},{5... | collective-permute-start | bytes 2654216 | tf_op jit(solution)/shard_map/ppermute | solution.py:657
  39.6 85.4 %collective-permute-start.5 = (bf16[384,1152]{1,0:T(8,128)(2,1)}, bf16[384,1152]{1,0:T(8,128)(2,1)}, u32[]{:S(2)}, u32[]{:S(2)}) collective-permute-start(bf16[384,1152]{1,0:T(8,128)(2,1)} %join.1.refs_2_), channel_id=1, source_target_pairs={{0,8},{4,12},{8,0},{12,4},{16,24},{20,28},{24,16},{28,20},{1,9},{5... | collective-permute-start | bytes 2654216 | tf_op jit(solution)/shard_map/ppermute | solution.py:657
  68.9 3.0 %collective-permute-start.3 = (s32[1,512]{1,0:T(1,128)S(1)}, s32[1,512]{1,0:T(1,128)S(1)}, u32[]{:S(2)}, u32[]{:S(2)}) collective-permute-start(s32[1,512]{1,0:T(1,128)S(1)} %copy-done.4), channel_id=1, source_target_pairs={{0,3},{1,2},{2,1},{3,0},{4,7},{5,6},{6,5},{7,4},{8,11},{9,10},{10,... | collective-permute-start | bytes 6152 | tf_op jit(solution)/shard_map/ppermute | solution.py:657
  68.9 24.5 %collective-permute-start.2 = (s32[1,512]{1,0:T(1,128)S(1)}, s32[1,512]{1,0:T(1,128)S(1)}, u32[]{:S(2)}, u32[]{:S(2)}) collective-permute-start(s32[1,512]{1,0:T(1,128)S(1)} %copy-done.4), channel_id=1, source_target_pairs={{0,2},{1,3},{2,0},{3,1},{4,6},{5,7},{6,4},{7,5},{8,10},{9,11},{10,... | collective-permute-start | bytes 6152 | tf_op jit(solution)/shard_map/ppermute | solution.py:657
  70.5 24.5 %collective-permute-start.1 = (s32[1,512]{1,0:T(1,128)S(1)}, s32[1,512]{1,0:T(1,128)S(1)}, u32[]{:S(2)}, u32[]{:S(2)}) collective-permute-start(s32[1,512]{1,0:T(1,128)S(1)} %copy-done.4), channel_id=1, source_target_pairs={{0,1},{1,0},{2,3},{3,2},{4,5},{5,4},{6,7},{7,6},{8,9},{9,8},{10,11... | collective-permute-start | bytes 6152 | tf_op jit(solution)/shard_map/ppermute | solution.py:657
  71.9 48.2 %collective-permute-start.9 = (bf16[96,3200]{1,0:T(8,128)(2,1)}, bf16[96,3200]{1,0:T(8,128)(2,1)}, u32[]{:S(2)}, u32[]{:S(2)}) collective-permute-start(bf16[96,3200]{1,0:T(8,128)(2,1)} %get-tuple-element.61), channel_id=1, source_target_pairs={{0,8},{4,12},{8,0},{12,4},{16,24},{20,28},{24,16},{28,20},{1,9},{5... | collective-permute-start | bytes 1843208 | tf_op jit(solution)/shard_map/ppermute | solution.py:657
  93.4 26.7 %collective-permute-start.10 = (bf16[96,3200]{1,0:T(8,128)(2,1)}, bf16[96,3200]{1,0:T(8,128)(2,1)}, u32[]{:S(2)}, u32[]{:S(2)}) collective-permute-start(bf16[96,3200]{1,0:T(8,128)(2,1)} %get-tuple-element.62), channel_id=1, source_target_pairs={{0,4},{4,0},{8,12},{12,8},{16,20},{20,16},{24,28},{28,24},{1,5},{5... | collective-permute-start | bytes 1843208 | tf_op jit(solution)/shard_map/ppermute | solution.py:657
  94.9 30.1 %collective-permute-start.11 = (bf16[96,3200]{1,0:T(8,128)(2,1)}, bf16[96,3200]{1,0:T(8,128)(2,1)}, u32[]{:S(2)}, u32[]{:S(2)}) collective-permute-start(bf16[96,3200]{1,0:T(8,128)(2,1)} %get-tuple-element.63), channel_id=1, source_target_pairs={{0,16},{4,20},{8,24},{12,28},{16,0},{20,4},{24,8},{28,12},{1,17},{... | collective-permute-start | bytes 1843208 | tf_op jit(solution)/shard_map/ppermute | solution.py:657
  125.1 42.1 %collective-permute-start.12 = (bf16[384,1152]{1,0:T(8,128)(2,1)}, bf16[384,1152]{1,0:T(8,128)(2,1)S(1)}, u32[]{:S(2)}, u32[]{:S(2)}) collective-permute-start(bf16[384,1152]{1,0:T(8,128)(2,1)} %collective-permute-done.5.refs_4_), channel_id=1, source_target_pairs={{0,4},{4,0},{8,12},{12,8},{16,20},{20,16},{24,28},{28,24},{1,5},{5... | collective-permute-start | bytes 2654216 | tf_op jit(solution)/shard_map/ppermute | solution.py:657
  125.6 41.6 %collective-permute-start.15 = (bf16[384,1152]{1,0:T(8,128)(2,1)}, bf16[384,1152]{1,0:T(8,128)(2,1)S(1)}, u32[]{:S(2)}, u32[]{:S(2)}) collective-permute-start(bf16[384,1152]{1,0:T(8,128)(2,1)} %join.1.refs_2_), channel_id=1, source_target_pairs={{0,16},{4,20},{8,24},{12,28},{16,0},{20,4},{24,8},{28,12},{1,17},{... | collective-permute-start | bytes 2654216 | tf_op jit(solution)/shard_map/ppermute | solution.py:657
  131.8 20.5 %collective-permute-start.14 = (bf16[128,3072]{1,0:T(8,128)(2,1)S(1)}, bf16[128,3072]{1,0:T(8,128)(2,1)S(1)}, u32[]{:S(2)}, u32[]{:S(2)}) collective-permute-start(bf16[128,3072]{1,0:T(8,128)(2,1)S(1)} %get-tuple-element.72), channel_id=1, source_target_pairs={{0,2},{1,3},{2,0},{3,1},{4,6},{5,7},{6,4},{7,5},{8,10},{9,11},{10,... | collective-permute-start | bytes 2359304 | tf_op jit(solution)/shard_map/ppermute | solution.py:657
  133.4 33.8 %collective-permute-start.13 = (bf16[128,3072]{1,0:T(8,128)(2,1)S(1)}, bf16[128,3072]{1,0:T(8,128)(2,1)S(1)}, u32[]{:S(2)}, u32[]{:S(2)}) collective-permute-start(bf16[128,3072]{1,0:T(8,128)(2,1)S(1)} %get-tuple-element.71), channel_id=1, source_target_pairs={{0,2},{1,3},{2,0},{3,1},{4,6},{5,7},{6,4},{7,5},{8,10},{9,11},{10,... | collective-permute-start | bytes 2359304 | tf_op jit(solution)/shard_map/ppermute | solution.py:657
  167.2 19.9 %collective-permute-start.19 = (bf16[384,1152]{1,0:T(8,128)(2,1)S(1)}, bf16[384,1152]{1,0:T(8,128)(2,1)S(1)}, u32[]{:S(2)}, u32[]{:S(2)}) collective-permute-start(bf16[384,1152]{1,0:T(8,128)(2,1)S(1)} %collective-permute-done.15.refs_6_), channel_id=1, source_target_pairs={{0,8},{4,12},{8,0},{12,4},{16,24},{20,28},{24,16},{28,20},{1,9},{5... | collective-permute-start | bytes 2654216 | tf_op jit(solution)/shard_map/ppermute | solution.py:657
  169.6 19.8 %collective-permute-start.18 = (bf16[384,1152]{1,0:T(8,128)(2,1)S(1)}, bf16[384,1152]{1,0:T(8,128)(2,1)S(1)}, u32[]{:S(2)}, u32[]{:S(2)}) collective-permute-start(bf16[384,1152]{1,0:T(8,128)(2,1)S(1)} %collective-permute-done.15.refs_6_), channel_id=1, source_target_pairs={{0,4},{4,0},{8,12},{12,8},{16,20},{20,16},{24,28},{28,24},{1,5},{5... | collective-permute-start | bytes 2654216 | tf_op jit(solution)/shard_map/ppermute | solution.py:657
  171.1 24.4 %collective-permute-start.16 = (bf16[128,3072]{1,0:T(8,128)(2,1)S(1)}, bf16[128,3072]{1,0:T(8,128)(2,1)S(1)}, u32[]{:S(2)}, u32[]{:S(2)}) collective-permute-start(bf16[128,3072]{1,0:T(8,128)(2,1)S(1)} %get-tuple-element.75), channel_id=1, source_target_pairs={{0,2},{1,3},{2,0},{3,1},{4,6},{5,7},{6,4},{7,5},{8,10},{9,11},{10,... | collective-permute-start | bytes 2359304 | tf_op jit(solution)/shard_map/ppermute | solution.py:657
  172.7 31.8 %collective-permute-start.17 = (bf16[128,3072]{1,0:T(8,128)(2,1)S(1)}, bf16[128,3072]{1,0:T(8,128)(2,1)S(1)}, u32[]{:S(2)}, u32[]{:S(2)}) collective-permute-start(bf16[128,3072]{1,0:T(8,128)(2,1)S(1)} %get-tuple-element.77), channel_id=1, source_target_pairs={{0,2},{1,3},{2,0},{3,1},{4,6},{5,7},{6,4},{7,5},{8,10},{9,11},{10,... | collective-permute-start | bytes 2359304 | tf_op jit(solution)/shard_map/ppermute | solution.py:657
  189.5 18.1 %collective-permute-start.20 = (bf16[384,1152]{1,0:T(8,128)(2,1)S(1)}, bf16[384,1152]{1,0:T(8,128)(2,1)S(1)}, u32[]{:S(2)}, u32[]{:S(2)}) collective-permute-start(bf16[384,1152]{1,0:T(8,128)(2,1)S(1)} %collective-permute-done.19.refs_8_), channel_id=1, source_target_pairs={{0,4},{4,0},{8,12},{12,8},{16,20},{20,16},{24,28},{28,24},{1,5},{5... | collective-permute-start | bytes 2654216 | tf_op jit(solution)/shard_map/ppermute | solution.py:657
  195.5 9.0 %collective-permute-start.23 = (bf16[128,3072]{1,0:T(8,128)(2,1)S(1)}, bf16[128,3072]{1,0:T(8,128)(2,1)S(1)}, u32[]{:S(2)}, u32[]{:S(2)}) collective-permute-start(bf16[128,3072]{1,0:T(8,128)(2,1)S(1)} %collective-permute-done.13.refs_2_), channel_id=1, source_target_pairs={{0,1},{1,0},{2,3},{3,2},{4,5},{5,4},{6,7},{7,6},{8,9},{9,8},{10,11... | collective-permute-start | bytes 2359304 | tf_op jit(solution)/shard_map/ppermute | solution.py:657
  195.6 22.3 %collective-permute-start.21 = (bf16[256,3072]{1,0:T(8,128)(2,1)S(1)}, bf16[256,3072]{1,0:T(8,128)(2,1)S(1)}, u32[]{:S(2)}, u32[]{:S(2)}) collective-permute-start(bf16[256,3072]{1,0:T(8,128)(2,1)S(1)} %get-tuple-element.84.refs_0_), channel_id=1, source_target_pairs={{0,1},{1,0},{2,3},{3,2},{4,5},{5,4},{6,7},{7,6},{8,9},{9,8},{10,11... | collective-permute-start | bytes 4718600 | tf_op jit(solution)/shard_map/ppermute | solution.py:657
  196.1 21.8 %collective-permute-start.22 = (bf16[256,3072]{1,0:T(8,128)(2,1)S(1)}, bf16[256,3072]{1,0:T(8,128)(2,1)S(1)}, u32[]{:S(2)}, u32[]{:S(2)}) collective-permute-start(bf16[256,3072]{1,0:T(8,128)(2,1)S(1)} %get-tuple-element.85.refs_1_), channel_id=1, source_target_pairs={{0,1},{1,0},{2,3},{3,2},{4,5},{5,4},{6,7},{7,6},{8,9},{9,8},{10,11... | collective-permute-start | bytes 4718600 | tf_op jit(solution)/shard_map/ppermute | solution.py:657
  204.5 13.3 %collective-permute-start.24 = (bf16[128,3072]{1,0:T(8,128)(2,1)S(1)}, bf16[128,3072]{1,0:T(8,128)(2,1)S(1)}, u32[]{:S(2)}, u32[]{:S(2)}) collective-permute-start(bf16[128,3072]{1,0:T(8,128)(2,1)S(1)} %collective-permute-done.14.refs_3_), channel_id=1, source_target_pairs={{0,1},{1,0},{2,3},{3,2},{4,5},{5,4},{6,7},{7,6},{8,9},{9,8},{10,11... | collective-permute-start | bytes 2359304 | tf_op jit(solution)/shard_map/ppermute | solution.py:657
  204.5 13.3 %collective-permute-start.25 = (bf16[128,3072]{1,0:T(8,128)(2,1)S(1)}, bf16[128,3072]{1,0:T(8,128)(2,1)S(1)}, u32[]{:S(2)}, u32[]{:S(2)}) collective-permute-start(bf16[128,3072]{1,0:T(8,128)(2,1)S(1)} %collective-permute-done.16.refs_4_), channel_id=1, source_target_pairs={{0,1},{1,0},{2,3},{3,2},{4,5},{5,4},{6,7},{7,6},{8,9},{9,8},{10,11... | collective-permute-start | bytes 2359304 | tf_op jit(solution)/shard_map/ppermute | solution.py:657
  207.5 10.3 %collective-permute-start.26 = (bf16[128,3072]{1,0:T(8,128)(2,1)S(1)}, bf16[128,3072]{1,0:T(8,128)(2,1)S(1)}, u32[]{:S(2)}, u32[]{:S(2)}) collective-permute-start(bf16[128,3072]{1,0:T(8,128)(2,1)S(1)} %collective-permute-done.17.refs_5_), channel_id=1, source_target_pairs={{0,1},{1,0},{2,3},{3,2},{4,5},{5,4},{6,7},{7,6},{8,9},{9,8},{10,11... | collective-permute-start | bytes 2359304 | tf_op jit(solution)/shard_map/ppermute | solution.py:657
  233.7 12.9 %collective-permute-start.29 = (bf16[512,384]{1,0:T(8,128)(2,1)S(1)}, bf16[512,384]{1,0:T(8,128)(2,1)S(1)}, u32[]{:S(2)}, u32[]{:S(2)}) collective-permute-start(bf16[512,384]{1,0:T(8,128)(2,1)S(1)} %get-tuple-element.97), channel_id=1, source_target_pairs={{0,2},{1,3},{2,0},{3,1},{4,6},{5,7},{6,4},{7,5},{8,10},{9,11},{10,... | collective-permute-start | bytes 1179656 | tf_op jit(solution)/shard_map/ppermute | solution.py:657
  236.7 18.0 %collective-permute-start.30 = (bf16[512,384]{1,0:T(8,128)(2,1)S(1)}, bf16[512,384]{1,0:T(8,128)(2,1)S(1)}, u32[]{:S(2)}, u32[]{:S(2)}) collective-permute-start(bf16[512,384]{1,0:T(8,128)(2,1)S(1)} %get-tuple-element.98), channel_id=1, source_target_pairs={{0,3},{1,2},{2,1},{3,0},{4,7},{5,6},{6,5},{7,4},{8,11},{9,10},{10,... | collective-permute-start | bytes 1179656 | tf_op jit(solution)/shard_map/ppermute | solution.py:657
  244.2 1.5 collective-permute-start.27
  244.3 1.7 collective-permute-start.28
